TPU v7x, 256 devices: a whole 4x4x8 slice. The times are simulated.
256 devices in a mesh: slab: 8 (over z_lo, y), vocab: 32 (over x, z_hi, core).
Axes of the slice: x: 4, y: 4, z: 8 (z_hi: 4, z_lo: 2; z = z_hi * 2 + z_lo), core: 2. Of those that a mesh axis runs over, the one named last changes fastest.
Arguments:
- teacher_ids: int32 [1024], replicated, may hold values from 0 to 152063
- slab_embed: bfloat16 [1024, 8192], P('slab', 'vocab'), may hold values from -2 to 2
- projection: bfloat16 [8192, 3072], P('vocab', 'slab'), may hold values from -0.0625 to 0.0625
- learner_vector_table: bfloat16 [65536, 3072], P('vocab', 'slab'), may hold values from -6 to 6
- teacher_dual: float32 [152064], replicated, may hold values from 1.055 to 1.08
- student_dual: float32 [65536], P('vocab'), may hold values from -0.05 to 0.05
Outputs:
- grad_projection: bfloat16 [8192, 3072], P('vocab', 'slab')
- grad_slab: bfloat16 [1024, 8192], P('slab', 'vocab')
- grad_student: bfloat16 [65536, 3072], P('vocab', 'slab')
All inputs are finite; a program needn't handle non-finite values.
Results may differ from a plain program's by a relative error of at most 0.0056.
Values may be sent and summed in bfloat16 or wider, within the bound.
A program may use at most 64 MiB of HBM per device.

v0:
```python
import jax
import jax.numpy as jnp
from jax import lax
from jax.sharding import PartitionSpec as P

DS = 3072


smoothing_strength = 0.04


def contract_first(left_op, right_op):
    return lax.dot_general(
        left_op, right_op, (((0,), (0,)), ((), ())), preferred_element_type=jnp.float32
    )


def contract_last(left_op, right_op):
    return lax.dot_general(
        left_op, right_op, (((1,), (1,)), ((), ())), preferred_element_type=jnp.float32
    )


def per_device(
    teacher_ids, slab_embed, projection, learner_vector_table, teacher_dual, student_dual
):
    slab_count = lax.axis_size("slab")
    vocab_count = lax.axis_size("vocab")
    slab_place = lax.axis_index("slab")
    local_rows = slab_embed.shape[0]
    source_marginal_mass = local_rows * slab_count
    local_vocab = learner_vector_table.shape[0]
    vocab_total = local_vocab * vocab_count
    gathered = lax.all_gather(slab_embed, "slab", axis=0, tiled=True)
    partial_proj = jnp.dot(gathered, projection, preferred_element_type=jnp.float32)
    projected = lax.psum(partial_proj, "vocab").astype(jnp.bfloat16)
    projected_f = projected.astype(jnp.float32)
    proj_square = jnp.sum(projected_f * projected_f, axis=1)
    embed_f = learner_vector_table.astype(jnp.float32)
    embed_square = jnp.sum(embed_f * embed_f, axis=1)
    source_dual_vector = teacher_dual[teacher_ids]
    column_count = local_vocab // slab_count
    embed_block = learner_vector_table
    inner = contract_last(embed_block, projected)
    pair_cost_transposed = lax.psum_scatter(
        (embed_square[:, None] + proj_square[None, :] - 2.0 * inner) / DS,
        "slab",
        scatter_dimension=0,
        tiled=True,
    )
    potential_block = lax.dynamic_slice_in_dim(
        student_dual, slab_place * column_count, column_count, 0
    )
    gibbs_kernel_transposed = jnp.exp(
        (potential_block[:, None] + source_dual_vector[None, :] - pair_cost_transposed)
        / smoothing_strength
    ).astype(jnp.bfloat16)
    portion = lax.all_gather(gibbs_kernel_transposed, "slab", axis=0, tiled=True)
    embed_block = learner_vector_table
    row_mass = jnp.sum(portion, axis=0, dtype=jnp.float32)
    row_acc = row_mass[:, None] * projected_f - contract_first(portion, embed_block)
    col_mass = jnp.sum(portion, axis=1, dtype=jnp.float32)
    student_rows = (
        col_mass[:, None] * embed_block.astype(jnp.float32)
        - jnp.dot(portion, projected, preferred_element_type=jnp.float32)
    ) / source_marginal_mass
    row_grad = (lax.psum(row_acc, "vocab") / vocab_total).astype(jnp.bfloat16)
    grad_slab = lax.psum_scatter(
        contract_last(row_grad, projection), "slab", scatter_dimension=0, tiled=True
    ).astype(jnp.bfloat16)
    grad_projection = (
        contract_first(gathered, row_grad) / jnp.sqrt(jnp.float32(source_marginal_mass))
    ).astype(jnp.bfloat16)
    return (grad_projection, grad_slab, student_rows.astype(jnp.bfloat16))


def solution(mesh):
    in_specs = (P(), P("slab", "vocab"), P("vocab", "slab"), P("vocab", "slab"), P(), P("vocab"))
    out_specs = (P("vocab", "slab"), P("slab", "vocab"), P("vocab", "slab"))
    return jax.shard_map(
        per_device, mesh=mesh, in_specs=in_specs, out_specs=out_specs, check_vma=False
    )
```

profile of v0, /device:TPU:1, one launch (start us, length us, event | category | flops | bytes accessed | tf_op | source)
XLA Modules:
  0.0 701.3 jit_solution(16947999532238510401)
XLA Ops:
  7.2 0.0 copy-start
  7.2 0.0 reduce-scatter.3.cloned.1.call-start
  7.2 25.1 %all_gather.6 = bf16[1024,256]{1,0:T(8,128)(2,1)S(1)} all-gather(bf16[128,256]{1,0:T(8,128)(2,1)} %param.7), channel_id=1, replica_groups=mesh['slab'=8,'vocab'=32] {'slab'}, dimensions={0}, use_global_device_ids=true | all-gather | bytes 589824 | tf_op jit(solution)/shard_map/all_gather | solution.py:34
  32.4 1.4 fusion.13
  33.7 159.0 %all-reduce.4 = bf16[1024,384]{1,0:T(8,128)(2,1)S(1)} all-reduce(f32[1024,384]{1,0:T(8,128)S(1)} %fusion.13), channel_id=1, replica_groups=mesh['slab'=8,'vocab'=32] {'vocab'}, use_global_device_ids=true, to_apply=%region_1.0 | all-reduce | flops 393216 | bytes 2359296 | tf_op jit(solution)/shard_map/psum | solution.py:36
  192.8 0.0 copy-start.3
  192.8 0.2 fusion.5
  193.0 1.9 fusion.1
  194.9 0.0 copy-done.3
  194.9 5.6 fusion
  200.5 0.0 copy-start.4
  200.6 0.0 reduce-scatter.3.cloned.1.call-update
  200.6 0.0 all-gather.2.cloned.1.call-start
  200.6 0.8 dynamic_slice.3
  201.4 0.0 copy-done.4
  201.4 0.0 copy-done
  201.4 6.2 gather_fusion
  207.6 87.5 %reduce-scatter.3.cloned.1.call-done = f32[256,1024]{0,1:T(8,128)} async-done(((f32[2048,1024]{0,1:T(8,128)}), f32[256,1024]{0,1:T(8,128)}) %reduce-scatter.3.cloned.1.call-update) | async-done | bytes 1048592 | tf_op jit(solution)/shard_map/reduce_scatter | solution.py:45
  295.1 2.3 exponential_convert_fusion
  297.4 0.0 all-gather.2.cloned.1.call-update
  297.4 0.0 all-reduce.3.cloned.1.call-start
  297.5 59.7 %all-gather.2.cloned.1.call-done = bf16[2048,1024]{0,1:T(8,128)(2,1)} async-done(((bf16[256,1024]{0,1:T(8,128)(2,1)}), bf16[2048,1024]{0,1:T(8,128)(2,1)}) %all-gather.2.cloned.1.call-update) | async-done | bytes 4194320 | tf_op jit(solution)/shard_map/all_gather | solution.py:58
  357.1 0.0 copy-start.2
  357.1 3.8 convert_reduce_fusion
  360.9 0.0 copy-done.2
  360.9 3.5 fusion.6
  364.4 0.0 all-reduce.3.cloned.1.call-update
  364.4 0.0 reduce-scatter.5.cloned.1.call-start
  364.5 289.8 %all-reduce.3.cloned.1.call-done = f32[1024,384]{1,0:T(8,128)} async-done(((f32[1024,384]{1,0:T(8,128)}), f32[1024,384]{1,0:T(8,128)}) %all-reduce.3.cloned.1.call-update) | async-done | bytes 1572880 | tf_op jit(solution)/shard_map/psum | solution.py:67
  654.2 2.9 fusion.9
  657.1 0.0 reduce-scatter.5.cloned.1.call-update
  657.1 0.0 copy-start.1
  657.1 5.9 fusion.4
  663.1 0.0 copy-done.1
  663.1 0.4 fusion.8
  663.5 0.8 copy.10
  664.3 28.9 %reduce-scatter.5.cloned.1.call-done = f32[128,256]{1,0:T(8,128)} async-done(((f32[1024,256]{1,0:T(8,128)}), f32[128,256]{1,0:T(8,128)}) %reduce-scatter.5.cloned.1.call-update) | async-done | bytes 131088 | tf_op jit(solution)/shard_map/reduce_scatter | solution.py:68
  693.2 1.5 convert_element_type.40
  (1 shorter events, 0.0 us)
Async XLA Ops:
  7.2 194.2 %copy-start = (f32[152064]{0:T(1024)S(1)}, f32[152064]{0:T(1024)}, u32[]{:S(2)}) copy-start(f32[152064]{0:T(1024)} %param.10) | copy-start | bytes 1824772
  7.2 287.9 %reduce-scatter.3.cloned.1.call-start = ((), (), s32[]{:S(2)}) async-start(), calls=%async_computation.2 | async-start | bytes 9437184 | tf_op jit(solution)/shard_map/reduce_scatter | solution.py:45
  192.8 2.2 copy-start.3
  200.5 0.8 copy-start.4
  200.6 156.6 %all-gather.2.cloned.1.call-start = ((), (), s32[]{:S(2)}) async-start(), calls=%async_computation.3 | async-start | bytes 4718592 | tf_op jit(solution)/shard_map/all_gather | solution.py:58
  297.4 356.8 %all-reduce.3.cloned.1.call-start = ((), (), s32[]{:S(2)}) async-start(), calls=%async_computation.4 | async-start | bytes 3145728 | tf_op jit(solution)/shard_map/psum | solution.py:67
  357.1 3.8 copy-start.2
  364.4 328.8 %reduce-scatter.5.cloned.1.call-start = ((), (), s32[]{:S(2)}) async-start(), calls=%async_computation.5 | async-start | bytes 1179648 | tf_op jit(solution)/shard_map/reduce_scatter | solution.py:68
  657.1 5.9 copy-start.1
Sparse Core Ops, SparseCore 0:
  200.7 94.3 reduce-scatter.2
  297.5 59.5 all-gather.1
  364.5 289.6 all-reduce.2
  657.2 35.9 reduce-scatter.4
where the time goes:
time: 706 us; the launch traced here: 701 us
  waiting for transfers between devices  466 us (66%)
  blocking collectives  184 us (26%)
  matrix products  19.7 us (3%)
  between operations  13.8 us (2%)
  other arithmetic  9.72 us (1%)
  local copies, waits for them, and re-layouts  7.76 us (1%)
    psum x1, waiting for transfers between devices, per_device(): row_grad = (lax.psum(row_acc, 'vocab') / vocab_total).astype(jnp.bfloat16)  290 us
    psum x1, blocking collectives, per_device(): projected = lax.psum(partial_proj, 'vocab').astype(jnp.bfloat16)  159 us
    reduce_scatter x1, waiting for transfers between devices, per_device(): lax.psum_scatter((embed_square[:, None] + proj_square[None, :] - 2.0 * in...  87.5 us
    all_gather x1, waiting for transfers between devices, per_device(): lax.all_gather(gibbs_kernel_transposed, 'slab', axis=0, tiled=True)  59.7 us
    reduce_scatter x1, waiting for transfers between devices, per_device(): lax.psum_scatter(contract_last(row_grad, projection), 'slab', scatter_dim...  28.9 us
    all_gather x1, blocking collectives, per_device(): gathered = lax.all_gather(slab_embed, 'slab', axis=0, tiled=True)  25.1 us
  transfers between devices with their start and end apart: 4, of which 4 were waited for; matrix products, arithmetic and copies ran while one was open for 2% of the time, Pallas kernels for 0%

commit v1 on v0

v1 whole, which is shorter than its diff:
```python
import jax
import jax.numpy as jnp
from jax import lax
from jax.experimental import pallas as pl
from jax.experimental.pallas import tpu as pltpu
from jax.sharding import PartitionSpec as P

DS = 3072
ROWS = 1024
VOCAB = 65536
STRENGTH = 0.04
FB = 384
DUAL_ROWS = 1280
NSEM = 112
F32, BF16 = jnp.float32, jnp.bfloat16
MESH = pl.DeviceIdType.MESH


def dot_last(a, b):
    return lax.dot_general(a, b, (((1,), (1,)), ((), ())), preferred_element_type=F32)


def dot_first(a, b):
    return lax.dot_general(a, b, (((0,), (0,)), ((), ())), preferred_element_type=F32)


def dot(a, b):
    return jnp.dot(a, b, preferred_element_type=F32)


def al(value, size):
    return pl.multiple_of(value, size)


def kernel(
    ids_ref, slab_ref, proj_ref, table_ref, dual_ref, sdual_ref,
    gp_ref, gs_ref, gst_ref,
    xg, sx, sdb, crecv, csend, acc, xsend, xrecv, zsend, zrecv, pown, pbuf,
    rd, qrow, kb, kt, rbuf, ra1, rb1, ra2, rb2, ra2r, rb2r, rz, rzr,
    rgown, rg, stsend, strecv, stown, gown, fsend, frecv,
    ssem, rsem, lsem,
):
    s = lax.axis_index("slab")
    v = lax.axis_index("vocab")
    zlo, y = lax.div(s, 4), lax.rem(s, 4)
    core, zhi, x = lax.rem(v, 2), lax.rem(lax.div(v, 2), 4), lax.div(v, 8)
    other = 1 - core

    def at_slab(d):
        return (lax.rem(s + d, 8), v)

    def at_x(d):
        return (s, lax.rem(x + d, 4) * 8 + zhi * 2 + core)

    def at_y(d):
        return (zlo * 4 + lax.rem(y + d, 4), v)

    def at_z(a, b):
        return (lax.rem(zlo + b, 2) * 4 + y, x * 8 + lax.rem(zhi + a, 4) * 2 + core)

    sibling = (s, x * 8 + zhi * 2 + other)
    z_peers = [(a, b) for a in range(4) for b in range(2) if a or b]

    used = [0]

    def send(src, dst, device):
        i = used[0]
        used[0] += 1
        copy = pltpu.make_async_remote_copy(
            src_ref=src, dst_ref=dst, send_sem=ssem.at[i], recv_sem=rsem.at[i],
            device_id=device, device_id_type=MESH,
        )
        copy.start()
        return copy

    sent = []

    def arrive(copies):
        for copy in copies:
            copy.wait_recv()
        sent.extend(copies)

    greet = [at_slab(d) for d in range(1, 8)] + [sibling] + [at_x(d) for d in range(1, 4)]
    greet += [at_z(a, b) for a, b in z_peers if a]
    barrier = pltpu.get_barrier_semaphore()
    for device in greet:
        pl.semaphore_signal(barrier, inc=1, device_id=device, device_id_type=MESH)
    pl.semaphore_wait(barrier, len(greet))

    mine = al(s * FB, FB)

    slabs = [send(slab_ref, xg.at[s], at_slab(d)) for d in range(1, 8)]
    xg[s] = slab_ref[...]
    students = []
    for d in range(1, 8):
        rows = al(lax.rem(s + d, 8) * 256, 256)
        students.append(send(table_ref.at[pl.ds(rows, 256), :], sx.at[0, :, pl.ds(mine, FB)], at_slab(d)))
    local = pltpu.make_async_copy(
        table_ref.at[pl.ds(al(s * 256, 256), 256), :], sx.at[0, :, pl.ds(mine, FB)], lsem.at[0]
    )
    local.start()
    duals = send(sdual_ref.at[s], sdb, sibling)

    ids = ids_ref[core]
    high, low = lax.div(ids, 128), lax.rem(ids, 128)
    found = jnp.zeros((128, 512), F32)
    step = 256
    for block in range(DUAL_ROWS // step):
        hot = (lax.broadcasted_iota(jnp.int32, (step, 512), 0) + block * step == high).astype(F32).astype(BF16)
        rest = dual_ref[block * step : (block + 1) * step, :]
        for _ in range(3):
            part = rest.astype(BF16)
            found += dot_first(part, hot)
            rest = rest - part.astype(F32)
    lane = lax.broadcasted_iota(jnp.int32, (128, 512), 0) == low
    row = jnp.sum(jnp.where(lane, found, 0.0), axis=0, keepdims=True)
    column = jnp.broadcast_to(row, (128, 512)).T
    rd[0] = column[:256]
    rd[1] = column[256:]

    arrive(slabs)
    for i in range(4):
        rows = slice((i % 2) * 128, (i % 2) * 128 + 128)
        csend[i // 2, rows, :] = dot(xg[other * 4 + i], proj_ref[...])
    pair = send(csend, crecv, sibling)
    for i in range(4):
        rows = slice((i % 2) * 128, (i % 2) * 128 + 128)
        acc[i // 2, rows, :] = dot(xg[core * 4 + i], proj_ref[...])
    arrive([pair])
    acc[...] += crecv[...]
    xsend[...] = acc[...].astype(BF16)
    copies = []
    for d in range(1, 4):
        rows = al(lax.rem(x + d, 4) * 64, 64)
        copies.append(send(xsend.at[:, pl.ds(rows, 64), :], xrecv.at[d - 1], at_x(d)))
    arrive(copies)
    total = acc[:, pl.ds(al(x * 64, 64), 64), :]
    for d in range(3):
        total += xrecv[d].astype(F32)
    zsend[...] = total
    copies = []
    for a in range(1, 4):
        rows = al(lax.rem(zhi + a, 4) * 16, 16)
        copies.append(send(zsend.at[:, pl.ds(rows, 16), :], zrecv.at[a - 1], at_z(a, 0)))
    arrive(copies)
    total = zsend[:, pl.ds(al(zhi * 16, 16), 16), :]
    for a in range(3):
        total += zrecv[a]
    pown[...] = total.astype(BF16)

    xrows = al(x * 64, 64)
    own_rows = al(x * 64 + zhi * 16, 16)
    copies = [send(pown, pbuf.at[:, pl.ds(own_rows, 16), pl.ds(mine, FB)], at_z(a, b)) for a, b in z_peers]
    keep = pltpu.make_async_copy(pown, pbuf.at[:, pl.ds(own_rows, 16), pl.ds(mine, FB)], lsem.at[1])
    keep.start()

    arrive(students)
    local.wait()
    both = send(sx.at[0], sx.at[1], sibling)

    keep.wait()
    arrive(copies)
    ycols = [al((z * 4 + y) * FB, FB) for z in range(2)]
    to_x, to_y = [], []
    for d in range(1, 4):
        for z in range(2):
            block = pbuf.at[0, pl.ds(xrows, 64), pl.ds(ycols[z], FB)]
            to_x.append(send(block, block, at_x(d)))
            block = pbuf.at[1, pl.ds(xrows, 64), pl.ds(ycols[z], FB)]
            to_y.append(send(block, block, at_y(d)))
    arrive(to_x)
    first = []
    for d in range(1, 4):
        for z in range(2):
            block = pbuf.at[0, :, pl.ds(ycols[z], FB)]
            first.append(send(block, block, at_y(d)))
    arrive(to_y)
    second = []
    for d in range(1, 4):
        block = pbuf.at[1, pl.ds(xrows, 64), :]
        second.append(send(block, block, at_x(d)))

    arrive([both, duals])
    for j in range(2):
        norm = jnp.zeros((256, 1), F32)
        for c in range(8):
            part = sx[j, :, c * FB : (c + 1) * FB].astype(F32)
            norm += jnp.sum(part * part, axis=1, keepdims=True)
        norm = jnp.broadcast_to(norm, (256, 128)).T[0:1]
        dual = sdual_ref[s] if j == 0 else sdb[...]
        qrow[j] = (dual - norm * (1.0 / DS)) * (1.0 / STRENGTH)

    def affinity(k):
        norm = jnp.zeros((256, 1), F32)
        for c in range(8):
            part = pbuf[k, :, c * FB : (c + 1) * FB].astype(F32)
            norm += jnp.sum(part * part, axis=1, keepdims=True)
        bias = (rd[k][:, 0:1] - norm * (1.0 / DS)) * (1.0 / STRENGTH)
        mass = jnp.zeros((256, 1), F32)
        for j in range(2):
            inner = dot_last(pbuf[k], sx[j])
            entry = jnp.exp(bias + qrow[j] + inner * (2.0 / (DS * STRENGTH))).astype(BF16)
            kb[k, j] = entry
            wide = entry.astype(F32)
            kt[k, j] = wide.T.astype(BF16)
            mass += jnp.sum(wide, axis=1, keepdims=True)

        @pl.loop(0, 8)
        def _(c):
            cols = pl.ds(al(c * FB, FB), FB)
            term = mass * pbuf[k, :, cols].astype(F32)
            term -= dot(kb[k, 0], sx[0, :, cols])
            term -= dot(kb[k, 1], sx[1, :, cols])
            rbuf[k, :, cols] = term.astype(BF16)

    arrive(first)
    affinity(0)
    to_y = []
    for d in range(1, 4):
        for z in range(2):
            cols = al((z * 4 + lax.rem(y + d, 4)) * FB, FB)
            to_y.append(send(rbuf.at[0, :, pl.ds(cols, FB)], ra1.at[d - 1, z], at_y(d)))
    arrive(second)
    affinity(1)
    to_x = []
    for d in range(1, 4):
        rows = al(lax.rem(x + d, 4) * 64, 64)
        to_x.append(send(rbuf.at[1, pl.ds(rows, 64), :], rb1.at[d - 1], at_x(d)))

    def student_term(j, cols, mass):
        term = mass * sx[j, :, cols].astype(F32)
        term -= dot(kt[0, j], pbuf[0, :, cols])
        return term - dot(kt[1, j], pbuf[1, :, cols])

    def student_mass(j):
        wide = kt[0, j].astype(F32) + kt[1, j].astype(F32)
        return jnp.sum(wide, axis=1, keepdims=True)

    mass1 = student_mass(1)

    @pl.loop(0, 8)
    def _(c):
        cols = pl.ds(al(c * FB, FB), FB)
        stsend[:, cols] = student_term(1, cols, mass1).astype(BF16)

    swap = send(stsend, strecv, sibling)
    mass0 = student_mass(0)

    @pl.loop(0, 8)
    def _(c):
        cols = pl.ds(al(c * FB, FB), FB)
        stown[:, cols] = student_term(0, cols, mass0)

    arrive(to_y)
    for z in range(2):
        total = rbuf[0, :, pl.ds(ycols[z], FB)].astype(F32)
        for d in range(3):
            total += ra1[d, z].astype(F32)
        ra2[z] = total.astype(BF16)
    to_x2 = []
    for d in range(1, 4):
        rows = al(lax.rem(x + d, 4) * 64, 64)
        to_x2.append(send(ra2.at[:, pl.ds(rows, 64), :], ra2r.at[d - 1], at_x(d)))
    arrive(to_x)
    total = rbuf[1, pl.ds(xrows, 64), :].astype(F32)
    for d in range(3):
        total += rb1[d].astype(F32)
    rb2[...] = total.astype(BF16)
    to_y2 = []
    for d in range(1, 4):
        for z in range(2):
            cols = al((z * 4 + lax.rem(y + d, 4)) * FB, FB)
            to_y2.append(send(rb2.at[:, pl.ds(cols, FB)], rb2r.at[d - 1, z], at_y(d)))

    arrive(to_x2)
    total = ra2[:, pl.ds(xrows, 64), :].astype(F32)
    for d in range(3):
        total += ra2r[d].astype(F32)
    rz[:, 0] = total.astype(BF16)
    arrive(to_y2)
    for z in range(2):
        total = rb2[:, pl.ds(ycols[z], FB)].astype(F32)
        for d in range(3):
            total += rb2r[d, z].astype(F32)
        rz[z, 1] = total.astype(BF16)
    copies = []
    for i, (a, b) in enumerate(z_peers):
        rows = al(lax.rem(zhi + a, 4) * 16, 16)
        copies.append(send(rz.at[lax.rem(zlo + b, 2), :, pl.ds(rows, 16), :], rzr.at[i], at_z(a, b)))

    arrive([swap])

    @pl.loop(0, 8)
    def _(c):
        cols = pl.ds(al(c * FB, FB), FB)
        gown[:, cols] = ((stown[:, cols] + strecv[:, cols].astype(F32)) * (1.0 / ROWS)).astype(BF16)

    arrive(copies)
    total = rz[zlo, :, pl.ds(al(zhi * 16, 16), 16), :].astype(F32)
    for i in range(7):
        total += rzr[i].astype(F32)
    rgown[...] = (total * (1.0 / VOCAB)).astype(BF16)
    copies = [send(rgown, rg.at[core, :, pl.ds(own_rows, 16), :], at_z(a, 0)) for a in range(1, 4)]
    rg[core, :, pl.ds(own_rows, 16), :] = rgown[...]

    srows = al(s * 256, 256)
    back = []
    for d in range(1, 8):
        cols = al(lax.rem(s + d, 8) * FB, FB)
        back.append(send(gown.at[:, pl.ds(cols, FB)], gst_ref.at[pl.ds(srows, 256), :], at_slab(d)))
    gst_ref[pl.ds(srows, 256), :] = gown[:, pl.ds(mine, FB)]

    arrive(copies)
    copies = []
    for d in range(1, 4):
        block = rg.at[core, :, pl.ds(xrows, 64), :]
        copies.append(send(block, block, at_x(d)))
    arrive(copies)
    pair = send(rg.at[core], rg.at[core], sibling)
    arrive([pair])

    def slab_term(index):
        half, k, rows = lax.div(index, 4), lax.rem(lax.div(index, 2), 2), al(lax.rem(index, 2) * 128, 128)
        return dot_last(rg[half, k, pl.ds(rows, 128), :], proj_ref[...])

    copies = []
    for d in range(1, 8):
        fsend[d - 1] = slab_term(lax.rem(s + d, 8)).astype(BF16)
        copies.append(send(fsend.at[d - 1], frecv.at[d - 1], at_slab(d)))
    own = slab_term(s)
    total = jnp.zeros((256, FB), F32)
    for i in range(8):
        half, k, rows = i // 4, (i // 2) % 2, (i % 2) * 128
        total += dot_first(xg[i], rg[half, k, rows : rows + 128, :])
    gp_ref[...] = (total * (1.0 / 32.0)).astype(BF16)
    arrive(copies)
    for d in range(7):
        own += frecv[d].astype(F32)
    gs_ref[...] = own.astype(BF16)

    arrive(back)
    for copy in sent:
        copy.wait_send()


def per_device(
    teacher_ids, slab_embed, projection, learner_vector_table, teacher_dual, student_dual
):
    ids = teacher_ids.reshape(2, 1, ROWS // 2)
    count = teacher_dual.shape[0]
    duals = jnp.pad(teacher_dual, (0, DUAL_ROWS * 128 - count)).reshape(DUAL_ROWS, 128)
    sdual = student_dual.reshape(8, 1, 256)
    vmem = pl.BlockSpec(memory_space=pltpu.VMEM)
    bf, ff = (lambda *n: pltpu.VMEM(n, BF16)), (lambda *n: pltpu.VMEM(n, F32))
    return pl.pallas_call(
        kernel,
        out_shape=(
            jax.ShapeDtypeStruct(projection.shape, BF16),
            jax.ShapeDtypeStruct(slab_embed.shape, BF16),
            jax.ShapeDtypeStruct(learner_vector_table.shape, BF16),
        ),
        in_specs=[vmem, vmem, vmem, pl.BlockSpec(memory_space=pl.ANY), vmem, vmem],
        out_specs=(vmem, vmem, vmem),
        scratch_shapes=[
            bf(8, 128, 256),
            bf(2, 256, DS),
            ff(1, 256),
            ff(2, 256, FB),
            ff(2, 256, FB),
            ff(2, 256, FB),
            bf(2, 256, FB),
            bf(3, 2, 64, FB),
            ff(2, 64, FB),
            ff(3, 2, 16, FB),
            bf(2, 16, FB),
            bf(2, 256, DS),
            ff(2, 256, 128),
            ff(2, 1, 256),
            bf(2, 2, 256, 256),
            bf(2, 2, 256, 256),
            bf(2, 256, DS),
            bf(3, 2, 256, FB),
            bf(3, 64, DS),
            bf(2, 256, FB),
            bf(64, DS),
            bf(3, 2, 64, FB),
            bf(3, 2, 64, FB),
            bf(2, 2, 64, FB),
            bf(7, 2, 16, FB),
            bf(2, 16, FB),
            bf(2, 2, 256, FB),
            bf(256, DS),
            bf(256, DS),
            ff(256, DS),
            bf(256, DS),
            bf(7, 128, 256),
            bf(7, 128, 256),
            pltpu.SemaphoreType.DMA((NSEM,)),
            pltpu.SemaphoreType.DMA((NSEM,)),
            pltpu.SemaphoreType.DMA((2,)),
        ],
        compiler_params=pltpu.CompilerParams(
            collective_id=0, has_side_effects=True, vmem_limit_bytes=56 * 1024 * 1024
        ),
        cost_estimate=pl.CostEstimate(flops=5_500_000_000, bytes_accessed=5_000_000, transcendentals=262144),
    )(ids, slab_embed, projection, learner_vector_table, duals, sdual)


def solution(mesh):
    in_specs = (P(), P("slab", "vocab"), P("vocab", "slab"), P("vocab", "slab"), P(), P("vocab"))
    out_specs = (P("vocab", "slab"), P("slab", "vocab"), P("vocab", "slab"))
    return jax.shard_map(
        per_device, mesh=mesh, in_specs=in_specs, out_specs=out_specs, check_vma=False
    )
```

time: 706 us -> 154 us (0.22)
  waiting for transfers between devices: 466 us -> 0 us
  blocking collectives: 184 us -> 0 us
  Pallas kernels: 0 us -> 145 us
  matrix products: 19.7 us -> 0 us
  between operations: 13.8 us -> 0.64 us
  other arithmetic: 9.72 us -> 0 us
    psum x1 -> x0, waiting for transfers between devices: 290 us -> none  [per_device(): row_grad = (lax.psum(row_acc, 'vocab') / vocab_total).astype(jnp.bfloat16)]
    psum x1 -> x0, blocking collectives: 159 us -> none  [per_device(): projected = lax.psum(partial_proj, 'vocab').astype(jnp.bfloat16)]
    pallas_call x0 -> x1, Pallas kernels: none -> 145 us  [per_device(): pl.pallas_call(kernel, out_shape=(jax.ShapeDtypeStruct(projection.shape,...]
    reduce_scatter x2 -> x0, waiting for transfers between devices: 116 us -> none  [the longest x1 87.5 us: per_device(): lax.psum_scatter((embed_square[:, None] + proj_square[None, :] - 2.0 * in...]
    all_gather x1 -> x0, waiting for transfers between devices: 59.7 us -> none  [per_device(): lax.all_gather(gibbs_kernel_transposed, 'slab', axis=0, tiled=True)]
    all_gather x1 -> x0, blocking collectives: 25.1 us -> none  [per_device(): gathered = lax.all_gather(slab_embed, 'slab', axis=0, tiled=True)]
    dot_general x6 -> x0, matrix products: 19.7 us -> none  [the longest x2 8.48 us: contract_last(): lax.dot_general(left_op, right_op, (((1,), (1,)), ((), ())), preferred_el...]
  transfers between devices with their start and end apart: 4 -> 0, of which waited for: 4 -> 0; matrix products, arithmetic and copies ran while one was open for 2% -> 0% of each run, Pallas kernels for 0% -> 0%
where the time goes in v1:
time: 154 us; the launch traced here: 153 us
  Pallas kernels  145 us (94%)
  local copies, waits for them, and re-layouts  7.75 us (5%)
    pallas_call x1, Pallas kernels, per_device(): pl.pallas_call(kernel, out_shape=(jax.ShapeDtypeStruct(projection.shape,...  145 us
    unnamed x3, local copies, waits for them, and re-layouts  5.8 us

profile of v1, /device:TPU:1, one launch (start us, length us, event | category | flops | bytes accessed | tf_op | source)
XLA Modules:
  0.0 153.5 jit_solution(13297988683615613809)
XLA Ops:
  0.6 2.0 %pad_bitcast_fusion.dual_ref = f32[1280,128]{1,0:T(8,128)} fusion(f32[152064]{0:T(1024)} %param.10), kind=kLoop, calls=%fused_computation | loop fusion | bytes 1263616 | tf_op jit(solution)/shard_map/reshape | solution.py:351
  2.6 145.1 %shard_map.85 = (bf16[256,384]{1,0:T(8,128)(2,1)}, bf16[128,256]{1,0:T(8,128)(2,1)}, bf16[2048,384]{1,0:T(8,128)(2,1)}) custom-call(s32[2,1,512]{2,1,0:T(1,128)} %bitcast.5, bf16[128,256]{1,0:T(8,128)(2,1)} %slab_ref.1, bf16[256,384]{1,0:T(8,128)(2,1)} %proj_ref.1, bf16[2048,384]{1,0:T(8,128)(2,1)} %table_ref.1, f32[1280,128]{1,0:T(8,128)} %pad_bitcast_fusion.dual_ref, ...), custom_call_target="tpu_custom_call" | custom-call | flops 5500000256 | bytes 5000000 | tf_op jit(solution)/shard_map/pallas_call | solution.py:355
  147.7 1.6 %copy.12 = bf16[256,384]{1,0:T(8,128)(2,1)} copy(bf16[256,384]{1,0:T(8,128)(2,1)} %get-tuple-element.6) | data formatting | bytes 393216
  149.3 1.5 copy.13
  150.8 2.7 %copy.14 = bf16[2048,384]{1,0:T(8,128)(2,1)} copy(bf16[2048,384]{1,0:T(8,128)(2,1)} %get-tuple-element.8) | data formatting | bytes 3145728

commit v2 on v0

v2 whole, which is shorter than its diff:
```python
import jax
import jax.numpy as jnp
from jax import lax
from jax.experimental import pallas as pl
from jax.experimental.pallas import tpu as pltpu
from jax.sharding import PartitionSpec as P

DS = 3072
ROWS = 1024
VOCAB = 65536
STRENGTH = 0.04
FB = 384
NSEM = 224
IN_FIRST, IN_LATER = ((1, 1), (3, 1), (1, 0), (3, 0), (2, 0)), ((2, 1), (0, 1))
OUT_FIRST, OUT_THEN, OUT_LATER = ((1, 1), (3, 1)), ((1, 0), (3, 0), (2, 0)), ((2, 1), (0, 1))
F32, BF16 = jnp.float32, jnp.bfloat16
MESH = pl.DeviceIdType.MESH


def dot_last(a, b):
    return lax.dot_general(a, b, (((1,), (1,)), ((), ())), preferred_element_type=F32)


def dot_first(a, b):
    return lax.dot_general(a, b, (((0,), (0,)), ((), ())), preferred_element_type=F32)


def dot(a, b):
    return jnp.dot(a, b, preferred_element_type=F32)


def al(value, size):
    return pl.multiple_of(value, size)


def kernel(
    ids_ref, slab_ref, proj_hbm, table_ref, dual_hbm, sdual_ref,
    gp_ref, gs_ref, gst_ref,
    proj_ref, dual_ref, xg, sx, sdb, crecv, csend, acc, xsend, xrecv, zsend, zrecv, pown, pbuf,
    dtail, rd, qrow, kb, kt, rbuf, rfirst, rlast, rmid, rgot, rz, rzr,
    rgown, rg, stsend, strecv, stown, gown, fsend, frecv,
    ssem, rsem, lsem,
):
    s = lax.axis_index("slab")
    v = lax.axis_index("vocab")
    zlo, y = lax.div(s, 4), lax.rem(s, 4)
    core, zhi, x = lax.rem(v, 2), lax.rem(lax.div(v, 2), 4), lax.div(v, 8)
    other, zother = 1 - core, 1 - zlo

    def at_slab(d):
        return (lax.rem(s + d, 8), v)

    def at_x(d):
        return (s, lax.rem(x + d, 4) * 8 + zhi * 2 + core)

    def at_y(d):
        return (zlo * 4 + lax.rem(y + d, 4), v)

    def at_yz(d, b):
        return (lax.rem(zlo + b, 2) * 4 + lax.rem(y + d, 4), v)

    def at_z(a, b):
        return (lax.rem(zlo + b, 2) * 4 + y, x * 8 + lax.rem(zhi + a, 4) * 2 + core)

    sibling = (s, x * 8 + zhi * 2 + other)
    slab_order = [(1, 1), (3, 1), (2, 1), (1, 0), (3, 0), (2, 0), (0, 1)]
    z_peers = [(a, b) for a in range(4) for b in range(2) if a or b]

    used = [0]
    sent = []

    def send(src, dst, device):
        i = used[0]
        used[0] += 1
        copy = pltpu.make_async_remote_copy(
            src_ref=src, dst_ref=dst, send_sem=ssem.at[i], recv_sem=rsem.at[i],
            device_id=device, device_id_type=MESH,
        )
        copy.start()
        return copy

    def arrive(copies):
        for copy in copies:
            copy.wait_recv()
        sent.extend(copies)

    class Gather:
        def __init__(self, view, index, at):
            self.view, self.index, self.at = view, index, at
            a, b = view(index, 0), view(index, 1)
            self.first = [send(a, a, at(1)), send(b, b, at(3))]
            self.rest = [send(b, b, at(1)), send(a, a, at(3))]

        def forward(self):
            arrive(self.first[:1])
            block = self.view(lax.rem(self.index + 3, 4), 0)
            self.rest.append(send(block, block, self.at(1)))
            arrive(self.first[1:])
            block = self.view(lax.rem(self.index + 1, 4), 1)
            self.rest.append(send(block, block, self.at(3)))

        def finish(self):
            arrive(self.rest)

    class Reduce:
        def __init__(self, view, index, at, first, last, own=None):
            self.view, self.index, self.at, self.first, self.last = view, index, at, first, last
            self.own = own or (lambda j, h: view(j, h)[...].astype(F32))
            right, left, far = [lax.rem(index + d, 4) for d in (1, 3, 2)]
            self.right, self.left = right, left
            self.head = [send(view(far, 0), first.at[0], at(1)), send(view(far, 1), first.at[1], at(3))]
            self.rest = [send(view(right, 1), last.at[0, 1], at(1)), send(view(left, 0), last.at[1, 0], at(3))]

        def forward(self):
            arrive(self.head[:1])
            block = self.view(self.right, 0)
            block[...] = (self.own(self.right, 0) + self.first[0].astype(F32)).astype(BF16)
            self.rest.append(send(block, self.last.at[0, 0], self.at(1)))
            arrive(self.head[1:])
            block = self.view(self.left, 1)
            block[...] = (self.own(self.left, 1) + self.first[1].astype(F32)).astype(BF16)
            self.rest.append(send(block, self.last.at[1, 1], self.at(3)))

        def finish(self):
            arrive(self.rest)

        def total(self, h):
            total = self.own(self.index, h) + self.last[0, h].astype(F32)
            return total + self.last[1, h].astype(F32)

    class Spread:
        def __init__(self, block, at):
            self.copies = [send(block, block, at(d)) for d in (1, 3, 2)]

        def finish(self):
            arrive(self.copies)

    class Collect:
        def __init__(self, view, index, at, got):
            self.got = got
            self.copies = [send(view(lax.rem(index + d, 4)), got.at[d - 1], at(d)) for d in (1, 3, 2)]

        def total(self, own):
            arrive(self.copies)
            for d in range(3):
                own += self.got[d].astype(F32)
            return own

    greet = [at_slab(d) for d in range(1, 8)] + [sibling] + [at_x(d) for d in (1, 2, 3)]
    greet += [at_z(a, b) for a, b in z_peers if a]
    barrier = pltpu.get_barrier_semaphore()
    for device in greet:
        pl.semaphore_signal(barrier, inc=1, device_id=device, device_id_type=MESH)
    pl.semaphore_wait(barrier, len(greet))

    mine = al(s * FB, FB)
    own_rows = pl.ds(al(zhi * 16, 16), 16)

    def yz(d, b):
        return lax.rem(zlo + b, 2) * 4 + lax.rem(y + d, 4)

    state = {}
    load_proj = pltpu.make_async_copy(proj_hbm, proj_ref, lsem.at[2])
    load_dual = pltpu.make_async_copy(dual_hbm, dual_ref, lsem.at[3])
    load_proj.start()
    load_dual.start()

    def rows_of(ref, k, c, u):
        return ref[k, c // 4, c % 4, :, u * 32 : u * 32 + 32, :].reshape(128, FB)

    def affinity(k, u):
        norm = jnp.zeros((128, 1), F32)
        for c in range(8):
            part = rows_of(pbuf, k, c, u).astype(F32)
            norm += jnp.sum(part * part, axis=1, keepdims=True)
        bias = rd[k, :, u * 32 : u * 32 + 32, 0:1].reshape(128, 1)
        bias = (bias - norm * (1.0 / DS)) * (1.0 / STRENGTH)
        mass = jnp.zeros((128, 1), F32)
        for j in range(2):
            inner = jnp.zeros((128, 256), F32)
            for c in range(8):
                inner += dot_last(rows_of(pbuf, k, c, u), sx[j, :, c * FB : (c + 1) * FB])
            entry = jnp.exp(bias + qrow[j] + inner * (2.0 / (DS * STRENGTH))).astype(BF16)
            kb[j] = entry
            wide = entry.astype(F32)
            kt[k, j, :, u * 128 : u * 128 + 128] = wide.T.astype(BF16)
            mass += jnp.sum(wide, axis=1, keepdims=True)
        for c in range(8):
            cols = slice(c * FB, (c + 1) * FB)
            term = mass * rows_of(pbuf, k, c, u).astype(F32)
            term -= dot(kb[0], sx[0, :, cols])
            term -= dot(kb[1], sx[1, :, cols])
            rbuf[k, c // 4, c % 4, :, u * 32 : u * 32 + 32, :] = term.astype(BF16).reshape(4, 32, FB)

    def slab_term(k, index):
        return dot_last(rg[lax.div(index, 4), k, lax.rem(index, 4)], proj_ref[...])

    def chain(k):
        index_mid, at_mid, index_last, at_last = (x, at_x, y, at_y) if k == 0 else (y, at_y, x, at_x)

        def block_of(ref, u):
            def view(j, h):
                rows = slice(u * 32 + h * 16, u * 32 + h * 16 + 16)
                return ref.at[0, :, j, :, rows, :] if k == 0 else ref.at[1, :, :, j, rows, :]

            return view

        whole = slice(k * 64, k * 64 + 64)
        copies = [send(slab_ref.at[whole, :], xg.at[s, whole, :], at_yz(d, b)) for d, b in slab_order]
        xg[s, whole, :] = slab_ref[whole, :]
        yield
        arrive(copies)
        if k == 0:
            load_proj.wait()
        for i in range(4):
            csend[k, i] = dot(xg[other * 4 + i, whole, :], proj_ref[...])
        pair = send(csend.at[k], crecv.at[k], sibling)
        for i in range(4):
            acc[k, i] = dot(xg[core * 4 + i, whole, :], proj_ref[...])
        yield
        arrive([pair])
        acc[k] = acc[k] + crecv[k]
        xsend[k] = acc[k].astype(BF16)
        collect = Collect(lambda j: xsend.at[k, j], x, at_x, xrecv.at[k])
        yield
        zsend[k] = collect.total(acc[k, x])
        copies = []
        for a in range(1, 4):
            rows = al(lax.rem(zhi + a, 4) * 16, 16)
            copies.append(send(zsend.at[k, pl.ds(rows, 16), :], zrecv.at[k, a - 1], at_z(a, 0)))
        yield
        arrive(copies)
        total = zsend[k, own_rows, :]
        for a in range(3):
            total += zrecv[k, a]
        pown[k] = total.astype(BF16)
        place = pbuf.at[k, zlo, y, x, own_rows, :]
        copies = [send(pown.at[k], place, at_z(a, b)) for a, b in z_peers]
        pbuf[k, zlo, y, x, own_rows, :] = pown[k]
        yield
        arrive(copies)
        spread = Spread(pbuf.at[k, :, y, x], at_mid)
        yield
        spread.finish()
        gathers = [Gather(block_of(pbuf, u), index_last, at_last) for u in range(2)]
        yield
        gathers[0].forward()
        yield
        gathers[1].forward()
        yield
        reduces = []
        for u in range(2):
            gathers[u].finish()
            affinity(k, u)
            reduces.append(Reduce(block_of(rbuf, u), index_last, at_last, rfirst.at[k, u], rlast.at[k, u]))
            yield
        reduces[0].forward()
        yield
        reduces[1].forward()
        yield
        for u in range(2):
            reduces[u].finish()
            for h in range(2):
                rmid[k, :, :, u * 32 + h * 16 : u * 32 + h * 16 + 16, :] = reduces[u].total(h).astype(BF16)
        collect = Collect(lambda j: rmid.at[k, :, j], index_mid, at_mid, rgot.at[k])
        yield
        rz[k] = collect.total(rmid[k, :, index_mid].astype(F32)).astype(BF16)
        copies = []
        for i, (a, b) in enumerate(z_peers):
            rows = al(lax.rem(zhi + a, 4) * 16, 16)
            copies.append(send(rz.at[k, lax.rem(zlo + b, 2), pl.ds(rows, 16), :], rzr.at[k, i], at_z(a, b)))
        yield
        arrive(copies)
        total = rz[k, zlo, own_rows, :].astype(F32)
        for i in range(7):
            total += rzr[k, i].astype(F32)
        rgown[k] = (total * (1.0 / VOCAB)).astype(BF16)
        copies = [send(rgown.at[k], rg.at[core, k, x, own_rows, :], at_z(a, 0)) for a in range(1, 4)]
        rg[core, k, x, own_rows, :] = rgown[k]
        yield
        arrive(copies)
        spread = Spread(rg.at[core, k, x], at_x)
        yield
        spread.finish()
        pair = send(rg.at[core, k], rg.at[core, k], sibling)
        yield
        arrive([pair])
        copies = []
        for i, (d, b) in enumerate(slab_order):
            fsend[k, i] = slab_term(k, yz(d, b)).astype(BF16)
            copies.append(send(fsend.at[k, i], frecv.at[k, i], at_yz(d, b)))
        yield
        total = slab_term(k, s)
        arrive(copies)
        for i in range(7):
            total += frecv[k, i].astype(F32)
        gs_ref[whole, :] = total.astype(BF16)
        yield

    def student_block(d, b):
        rows = al(yz(d, b) * 256, 256)
        return send(table_ref.at[pl.ds(rows, 256), :], sx.at[0, :, pl.ds(mine, FB)], at_yz(d, b))

    def students_start():
        state["students"] = [student_block(d, b) for d, b in IN_FIRST]
        state["local"] = pltpu.make_async_copy(
            table_ref.at[pl.ds(al(s * 256, 256), 256), :], sx.at[0, :, pl.ds(mine, FB)], lsem.at[0]
        )
        state["local"].start()
        state["duals"] = send(sdual_ref.at[s], sdb, sibling)

    def students_across():
        state["students"] += [student_block(d, b) for d, b in IN_LATER]

    def students_swap():
        arrive(state["students"])
        state["local"].wait()
        state["both"] = send(sx.at[0], sx.at[1], sibling)

    def teacher_duals():
        ids = ids_ref[core]
        high, low = lax.div(ids, 128), lax.rem(ids, 128)
        found = jnp.zeros((128, 512), F32)
        load_dual.wait()
        dtail[...] = jnp.zeros_like(dtail)
        whole = dual_ref.shape[0] // 16 * 16
        dtail[0 : dual_ref.shape[0] - whole, :] = dual_ref[whole:, :]
        half = whole // 2
        for base, rest in ((0, dual_ref[0:half, :]), (half, dual_ref[half:whole, :]), (whole, dtail[...])):
            hot = lax.broadcasted_iota(jnp.int32, (rest.shape[0], 512), 0) + base == high
            hot = hot.astype(F32).astype(BF16)
            for _ in range(3):
                part = rest.astype(BF16)
                found += dot_first(part, hot)
                rest = rest - part.astype(F32)
        lane = lax.broadcasted_iota(jnp.int32, (128, 512), 0) == low
        row = jnp.sum(jnp.where(lane, found, 0.0), axis=0, keepdims=True)
        column = jnp.broadcast_to(row, (128, 512)).T
        for k in range(2):
            for i in range(4):
                rd[k, i] = column[i * 128 + k * 64 : i * 128 + k * 64 + 64]

    def student_norms():
        arrive([state["both"], state["duals"]])
        for j in range(2):
            norm = jnp.zeros((256, 1), F32)
            for c in range(8):
                part = sx[j, :, c * FB : (c + 1) * FB].astype(F32)
                norm += jnp.sum(part * part, axis=1, keepdims=True)
            norm = jnp.broadcast_to(norm, (256, 128)).T[0:1]
            dual = sdual_ref[s] if j == 0 else sdb[...]
            qrow[j] = (dual - norm * (1.0 / DS)) * (1.0 / STRENGTH)

    def student_term(j, c, mass):
        cols = slice(c * FB, (c + 1) * FB)
        term = mass * sx[j, :, cols].astype(F32)
        for k in range(2):
            rows = jnp.concatenate([rows_of(pbuf, k, c, u) for u in range(2)], axis=0)
            term -= dot(kt[k, j], rows)
        return cols, term

    def student_mass(j):
        wide = kt[0, j].astype(F32) + kt[1, j].astype(F32)
        return jnp.sum(wide, axis=1, keepdims=True)

    def student_swap():
        mass = student_mass(1)

        for c in range(8):
            cols, term = student_term(1, c, mass)
            stsend[:, cols] = term.astype(BF16)

        state["swap"] = send(stsend, strecv, sibling)

    def student_own():
        mass = student_mass(0)

        for c in range(8):
            cols, term = student_term(0, c, mass)
            stown[:, cols] = term

    srows = al(s * 256, 256)

    def student_out(places):
        for d, b in places:
            cols = pl.ds(al(yz(d, b) * FB, FB), FB)
            state["back"].append(
                send(gown.at[:, cols], gst_ref.at[pl.ds(srows, 256), :], at_yz(d, b))
            )

    def student_back():
        arrive([state["swap"]])

        @pl.loop(0, 8)
        def _(c):
            cols = pl.ds(al(c * FB, FB), FB)
            gown[:, cols] = ((stown[:, cols] + strecv[:, cols].astype(F32)) * (1.0 / ROWS)).astype(BF16)

        state["back"] = []
        student_out(OUT_FIRST)
        state["keep"] = pltpu.make_async_copy(
            gown.at[:, pl.ds(mine, FB)], gst_ref.at[pl.ds(srows, 256), :], lsem.at[1]
        )
        state["keep"].start()

    def projection_gradient():
        total = jnp.zeros((256, FB), F32)
        for i in range(8):
            grad = jnp.concatenate([rg[i // 4, 0, i % 4], rg[i // 4, 1, i % 4]], axis=0)
            total += dot_first(xg[i], grad)
        gp_ref[...] = (total * (1.0 / 32.0)).astype(BF16)

    aside = {
        1: [students_start],
        2: [teacher_duals],
        5: [students_across],
        6: [students_swap],
        8: [student_norms],
        10: [student_swap],
        11: [student_own, student_back],
        14: [lambda: student_out(OUT_THEN)],
        16: [lambda: student_out(OUT_LATER)],
        18: [projection_gradient],
    }
    chains = [chain(0), chain(1)]
    for stage in range(20):
        for one in chains:
            next(one)
        for work in aside.get(stage, []):
            work()

    arrive(state["back"])
    state["keep"].wait()
    for copy in sent:
        copy.wait_send()


def deliver(gp_in, gs_in, gst_in, gp_ref, gs_ref, gst_ref, gp, gs, gst, sem):
    moves = [(gp_in, gp, gp_ref), (gs_in, gs, gs_ref)]
    part = gst_in.shape[0] // 4
    for i in range(4):
        rows = pl.ds(i * part, part)
        moves.append((gst_in.at[rows], gst.at[rows], gst_ref.at[rows]))
    loads = [pltpu.make_async_copy(a, b, sem.at[0, i]) for i, (a, b, _) in enumerate(moves)]
    stores = [pltpu.make_async_copy(b, c, sem.at[1, i]) for i, (_, b, c) in enumerate(moves)]
    for load in loads:
        load.start()
    for load, store in zip(loads, stores):
        load.wait()
        store.start()
    for store in stores:
        store.wait()


def per_device(
    teacher_ids, slab_embed, projection, learner_vector_table, teacher_dual, student_dual
):
    ids = teacher_ids.reshape(2, 1, ROWS // 2)
    duals = teacher_dual.reshape(teacher_dual.shape[0] // 128, 128)
    sdual = student_dual.reshape(8, 1, 256)
    vmem = pl.BlockSpec(memory_space=pltpu.VMEM)
    bf, ff = (lambda *n: pltpu.VMEM(n, BF16)), (lambda *n: pltpu.VMEM(n, F32))
    anywhere = pl.BlockSpec(memory_space=pl.ANY)
    shapes = (
        jax.ShapeDtypeStruct(projection.shape, BF16),
        jax.ShapeDtypeStruct(slab_embed.shape, BF16),
        jax.ShapeDtypeStruct(learner_vector_table.shape, BF16),
    )
    results = pl.pallas_call(
        kernel,
        out_shape=shapes,
        in_specs=[vmem, vmem, anywhere, anywhere, anywhere, vmem],
        out_specs=(vmem, vmem, anywhere),
        scratch_shapes=[
            pltpu.VMEM(projection.shape, BF16),
            pltpu.VMEM(duals.shape, F32),
            bf(8, 128, 256),
            bf(2, 256, DS),
            ff(1, 256),
            ff(2, 4, 64, FB),
            ff(2, 4, 64, FB),
            ff(2, 4, 64, FB),
            bf(2, 4, 64, FB),
            bf(2, 3, 64, FB),
            ff(2, 64, FB),
            ff(2, 3, 16, FB),
            bf(2, 16, FB),
            bf(2, 2, 4, 4, 64, FB),
            ff(16, 128),
            ff(2, 4, 64, 128),
            ff(2, 1, 256),
            bf(2, 128, 256),
            bf(2, 2, 256, 256),
            bf(2, 2, 4, 4, 64, FB),
            bf(2, 2, 2, 2, 4, 16, FB),
            bf(2, 2, 2, 2, 2, 4, 16, FB),
            bf(2, 2, 4, 64, FB),
            bf(2, 3, 2, 64, FB),
            bf(2, 2, 64, FB),
            bf(2, 7, 16, FB),
            bf(2, 16, FB),
            bf(2, 2, 4, 64, FB),
            bf(256, DS),
            bf(256, DS),
            ff(256, DS),
            bf(256, DS),
            bf(2, 7, 64, 256),
            bf(2, 7, 64, 256),
            pltpu.SemaphoreType.DMA((NSEM,)),
            pltpu.SemaphoreType.DMA((NSEM,)),
            pltpu.SemaphoreType.DMA((4,)),
        ],
        compiler_params=pltpu.CompilerParams(
            collective_id=0, has_side_effects=True, vmem_limit_bytes=56 * 1024 * 1024
        ),
        cost_estimate=pl.CostEstimate(flops=5_500_000_000, bytes_accessed=5_000_000, transcendentals=262144),
    )(ids, slab_embed, projection, learner_vector_table, duals, sdual)
    return pl.pallas_call(
        deliver,
        out_shape=shapes,
        in_specs=[anywhere] * 3,
        out_specs=(anywhere,) * 3,
        scratch_shapes=[pltpu.VMEM(shape.shape, BF16) for shape in shapes] + [pltpu.SemaphoreType.DMA((2, 6))],
        compiler_params=pltpu.CompilerParams(vmem_limit_bytes=60 * 1024 * 1024),
    )(*results)


def solution(mesh):
    in_specs = (P(), P("slab", "vocab"), P("vocab", "slab"), P("vocab", "slab"), P(), P("vocab"))
    out_specs = (P("vocab", "slab"), P("slab", "vocab"), P("vocab", "slab"))
    return jax.shard_map(
        per_device, mesh=mesh, in_specs=in_specs, out_specs=out_specs, check_vma=False
    )
```

time: 706 us -> 120 us (0.17)
  waiting for transfers between devices: 466 us -> 0 us
  blocking collectives: 184 us -> 0 us
  Pallas kernels: 0 us -> 119 us
  matrix products: 19.7 us -> 0 us
  between operations: 13.8 us -> 0.8 us
  other arithmetic: 9.72 us -> 0 us
  local copies, waits for them, and re-layouts: 7.76 us -> 0 us
    psum x1 -> x0, waiting for transfers between devices: 290 us -> none  [per_device(): row_grad = (lax.psum(row_acc, 'vocab') / vocab_total).astype(jnp.bfloat16)]
    psum x1 -> x0, blocking collectives: 159 us -> none  [per_device(): projected = lax.psum(partial_proj, 'vocab').astype(jnp.bfloat16)]
    pallas_call x0 -> x2, Pallas kernels: none -> 119 us  [the longest x1 116 us: per_device(): pl.pallas_call(kernel, out_shape=shapes, in_specs=[vmem, vmem, anywhere,...]
    reduce_scatter x2 -> x0, waiting for transfers between devices: 116 us -> none  [the longest x1 87.5 us: per_device(): lax.psum_scatter((embed_square[:, None] + proj_square[None, :] - 2.0 * in...]
    all_gather x1 -> x0, waiting for transfers between devices: 59.7 us -> none  [per_device(): lax.all_gather(gibbs_kernel_transposed, 'slab', axis=0, tiled=True)]
    all_gather x1 -> x0, blocking collectives: 25.1 us -> none  [per_device(): gathered = lax.all_gather(slab_embed, 'slab', axis=0, tiled=True)]
    dot_general x6 -> x0, matrix products: 19.7 us -> none  [the longest x2 8.48 us: contract_last(): lax.dot_general(left_op, right_op, (((1,), (1,)), ((), ())), preferred_el...]
  transfers between devices with their start and end apart: 4 -> 0, of which waited for: 4 -> 0; matrix products, arithmetic and copies ran while one was open for 2% -> 0% of each run, Pallas kernels for 0% -> 0%
where the time goes in v2:
time: 120 us; the launch traced here: 119 us
  Pallas kernels  119 us (99%)
    pallas_call x1, Pallas kernels, per_device(): pl.pallas_call(kernel, out_shape=shapes, in_specs=[vmem, vmem, anywhere,...  116 us

profile of v2, /device:TPU:1, one launch (start us, length us, event | category | flops | bytes accessed | tf_op | source)
XLA Modules:
  0.0 119.4 jit_solution(3040090338393576392)
XLA Ops:
  0.6 116.3 %shard_map.85 = (bf16[256,384]{1,0:T(8,128)(2,1)}, bf16[128,256]{1,0:T(8,128)(2,1)}, bf16[2048,384]{1,0:T(8,128)(2,1)}) custom-call(s32[2,1,512]{2,1,0:T(1,128)} %bitcast.5, bf16[128,256]{1,0:T(8,128)(2,1)} %slab_ref.1, bf16[256,384]{1,0:T(8,128)(2,1)} %proj_hbm.1, bf16[2048,384]{1,0:T(8,128)(2,1)} %table_ref.1, f32[1188,128]{1,0:T(8,128)} %bitcast.3, ...), custom_call_target="tpu_custom_call" | custom-call | flops 5500000256 | bytes 5000000 | tf_op jit(solution)/shard_map/pallas_call | solution.py:469
  116.9 2.4 %shard_map.86 = (bf16[256,384]{1,0:T(8,128)(2,1)}, bf16[128,256]{1,0:T(8,128)(2,1)}, bf16[2048,384]{1,0:T(8,128)(2,1)}) custom-call(bf16[256,384]{1,0:T(8,128)(2,1)} %get-tuple-element.6.gp_in, bf16[128,256]{1,0:T(8,128)(2,1)} %get-tuple-element.7.gs_in, bf16[2048,384]{1,0:T(8,128)(2,1)} %get-tuple-element.8.gst_in), custom_call_target="tpu_custom_call" | custom-call | tf_op jit(solution)/shard_map/pallas_call | solution.py:518

commit v3 on v2

--- a/solution.py
+++ b/solution.py
@@ -166,11 +166,13 @@
     load_dual.start()
 
     def rows_of(ref, k, c, u):
-        return ref[k, c // 4, c % 4, :, u * 32 : u * 32 + 32, :].reshape(128, FB)
+        rows = slice(u * 32, u * 32 + 32)
+        pair = [ref[k, i // 4, i % 4, :, rows, :].reshape(128, FB) for i in (2 * c, 2 * c + 1)]
+        return jnp.concatenate(pair, axis=1)
 
     def affinity(k, u):
         norm = jnp.zeros((128, 1), F32)
-        for c in range(8):
+        for c in range(4):
             part = rows_of(pbuf, k, c, u).astype(F32)
             norm += jnp.sum(part * part, axis=1, keepdims=True)
         bias = rd[k, :, u * 32 : u * 32 + 32, 0:1].reshape(128, 1)
@@ -178,19 +180,21 @@
         mass = jnp.zeros((128, 1), F32)
         for j in range(2):
             inner = jnp.zeros((128, 256), F32)
-            for c in range(8):
-                inner += dot_last(rows_of(pbuf, k, c, u), sx[j, :, c * FB : (c + 1) * FB])
+            for c in range(4):
+                inner += dot_last(rows_of(pbuf, k, c, u), sx[j, :, c * 2 * FB : (c + 1) * 2 * FB])
             entry = jnp.exp(bias + qrow[j] + inner * (2.0 / (DS * STRENGTH))).astype(BF16)
             kb[j] = entry
             wide = entry.astype(F32)
             kt[k, j, :, u * 128 : u * 128 + 128] = wide.T.astype(BF16)
             mass += jnp.sum(wide, axis=1, keepdims=True)
-        for c in range(8):
-            cols = slice(c * FB, (c + 1) * FB)
+        for c in range(4):
+            cols = slice(c * 2 * FB, (c + 1) * 2 * FB)
             term = mass * rows_of(pbuf, k, c, u).astype(F32)
             term -= dot(kb[0], sx[0, :, cols])
             term -= dot(kb[1], sx[1, :, cols])
-            rbuf[k, c // 4, c % 4, :, u * 32 : u * 32 + 32, :] = term.astype(BF16).reshape(4, 32, FB)
+            for i in range(2):
+                part = term[:, i * FB : (i + 1) * FB].astype(BF16).reshape(4, 32, FB)
+                rbuf[k, (2 * c + i) // 4, (2 * c + i) % 4, :, u * 32 : u * 32 + 32, :] = part
 
     def slab_term(k, index):
         return dot_last(rg[lax.div(index, 4), k, lax.rem(index, 4)], proj_ref[...])
@@ -223,16 +227,16 @@
         xsend[k] = acc[k].astype(BF16)
         collect = Collect(lambda j: xsend.at[k, j], x, at_x, xrecv.at[k])
         yield
-        zsend[k] = collect.total(acc[k, x])
+        zsend[k] = collect.total(acc[k, x]).astype(BF16)
         copies = []
         for a in range(1, 4):
             rows = al(lax.rem(zhi + a, 4) * 16, 16)
             copies.append(send(zsend.at[k, pl.ds(rows, 16), :], zrecv.at[k, a - 1], at_z(a, 0)))
         yield
         arrive(copies)
-        total = zsend[k, own_rows, :]
+        total = zsend[k, own_rows, :].astype(F32)
         for a in range(3):
-            total += zrecv[k, a]
+            total += zrecv[k, a].astype(F32)
         pown[k] = total.astype(BF16)
         place = pbuf.at[k, zlo, y, x, own_rows, :]
         copies = [send(pown.at[k], place, at_z(a, b)) for a, b in z_peers]
@@ -352,7 +356,7 @@
             qrow[j] = (dual - norm * (1.0 / DS)) * (1.0 / STRENGTH)
 
     def student_term(j, c, mass):
-        cols = slice(c * FB, (c + 1) * FB)
+        cols = slice(c * 2 * FB, (c + 1) * 2 * FB)
         term = mass * sx[j, :, cols].astype(F32)
         for k in range(2):
             rows = jnp.concatenate([rows_of(pbuf, k, c, u) for u in range(2)], axis=0)
@@ -366,7 +370,7 @@
     def student_swap():
         mass = student_mass(1)
 
-        for c in range(8):
+        for c in range(4):
             cols, term = student_term(1, c, mass)
             stsend[:, cols] = term.astype(BF16)
 
@@ -375,7 +379,7 @@
     def student_own():
         mass = student_mass(0)
 
-        for c in range(8):
+        for c in range(4):
             cols, term = student_term(0, c, mass)
             stown[:, cols] = term
 
@@ -413,11 +417,11 @@
     aside = {
         1: [students_start],
         2: [teacher_duals],
-        5: [students_across],
+        4: [students_across],
         6: [students_swap],
         8: [student_norms],
-        10: [student_swap],
-        11: [student_own, student_back],
+        10: [student_swap, student_own],
+        12: [student_back],
         14: [lambda: student_out(OUT_THEN)],
         16: [lambda: student_out(OUT_LATER)],
         18: [projection_gradient],
@@ -482,8 +486,8 @@
             ff(2, 4, 64, FB),
             bf(2, 4, 64, FB),
             bf(2, 3, 64, FB),
-            ff(2, 64, FB),
-            ff(2, 3, 16, FB),
+            bf(2, 64, FB),
+            bf(2, 3, 16, FB),
             bf(2, 16, FB),
             bf(2, 2, 4, 4, 64, FB),
             ff(16, 128),

time: 120 us -> 115 us (0.958)
  Pallas kernels: 119 us -> 114 us
    pallas_call x1, Pallas kernels: 116 us -> 112 us  [per_device(): pl.pallas_call(kernel, out_shape=shapes, in_specs=[vmem, vmem, anywhere,...]
where the time goes in v3:
time: 115 us
  Pallas kernels  114 us (99%)
    pallas_call x1, Pallas kernels, per_device(): pl.pallas_call(kernel, out_shape=shapes, in_specs=[vmem, vmem, anywhere,...  112 us
    pallas_call x1, Pallas kernels, per_device(): pl.pallas_call(deliver, out_shape=shapes, in_specs=[anywhere] * 3, out_sp...  2.37 us

profile of v3, /device:TPU:1, one launch (start us, length us, event | category | flops | bytes accessed | tf_op | source)
XLA Modules:
  0.0 114.8 jit_solution(8063407987966046133)
XLA Ops:
  0.6 111.6 %shard_map.85 = (bf16[256,384]{1,0:T(8,128)(2,1)}, bf16[128,256]{1,0:T(8,128)(2,1)}, bf16[2048,384]{1,0:T(8,128)(2,1)}) custom-call(s32[2,1,512]{2,1,0:T(1,128)} %bitcast.5, bf16[128,256]{1,0:T(8,128)(2,1)} %slab_ref.1, bf16[256,384]{1,0:T(8,128)(2,1)} %proj_hbm.1, bf16[2048,384]{1,0:T(8,128)(2,1)} %table_ref.1, f32[1188,128]{1,0:T(8,128)} %bitcast.3, ...), custom_call_target="tpu_custom_call" | custom-call | flops 5500000256 | bytes 5000000 | tf_op jit(solution)/shard_map/pallas_call | solution.py:473
  112.3 2.4 %shard_map.86 = (bf16[256,384]{1,0:T(8,128)(2,1)}, bf16[128,256]{1,0:T(8,128)(2,1)}, bf16[2048,384]{1,0:T(8,128)(2,1)}) custom-call(bf16[256,384]{1,0:T(8,128)(2,1)} %get-tuple-element.6.gp_in, bf16[128,256]{1,0:T(8,128)(2,1)} %get-tuple-element.7.gs_in, bf16[2048,384]{1,0:T(8,128)(2,1)} %get-tuple-element.8.gst_in), custom_call_target="tpu_custom_call" | custom-call | tf_op jit(solution)/shard_map/pallas_call | solution.py:522

commit v4 on v3

--- a/solution.py
+++ b/solution.py
@@ -63,8 +63,8 @@
         return (lax.rem(zlo + b, 2) * 4 + y, x * 8 + lax.rem(zhi + a, 4) * 2 + core)
 
     sibling = (s, x * 8 + zhi * 2 + other)
-    slab_order = [(1, 1), (3, 1), (2, 1), (1, 0), (3, 0), (2, 0), (0, 1)]
-    z_peers = [(a, b) for a in range(4) for b in range(2) if a or b]
+    slab_order = [(2, 1), (1, 1), (3, 1), (2, 0), (1, 0), (3, 0), (0, 1)]
+    z_peers = [(a, b) for a in (2, 1, 3, 0) for b in range(2) if a or b]
 
     used = [0]
     sent = []
@@ -130,7 +130,7 @@
 
     class Spread:
         def __init__(self, block, at):
-            self.copies = [send(block, block, at(d)) for d in (1, 3, 2)]
+            self.copies = [send(block, block, at(d)) for d in (2, 1, 3)]
 
         def finish(self):
             arrive(self.copies)
@@ -138,7 +138,7 @@
     class Collect:
         def __init__(self, view, index, at, got):
             self.got = got
-            self.copies = [send(view(lax.rem(index + d, 4)), got.at[d - 1], at(d)) for d in (1, 3, 2)]
+            self.copies = [send(view(lax.rem(index + d, 4)), got.at[d - 1], at(d)) for d in (2, 1, 3)]
 
         def total(self, own):
             arrive(self.copies)
@@ -229,7 +229,7 @@
         yield
         zsend[k] = collect.total(acc[k, x]).astype(BF16)
         copies = []
-        for a in range(1, 4):
+        for a in (2, 1, 3):
             rows = al(lax.rem(zhi + a, 4) * 16, 16)
             copies.append(send(zsend.at[k, pl.ds(rows, 16), :], zrecv.at[k, a - 1], at_z(a, 0)))
         yield
@@ -279,7 +279,7 @@
         for i in range(7):
             total += rzr[k, i].astype(F32)
         rgown[k] = (total * (1.0 / VOCAB)).astype(BF16)
-        copies = [send(rgown.at[k], rg.at[core, k, x, own_rows, :], at_z(a, 0)) for a in range(1, 4)]
+        copies = [send(rgown.at[k], rg.at[core, k, x, own_rows, :], at_z(a, 0)) for a in (2, 1, 3)]
         rg[core, k, x, own_rows, :] = rgown[k]
         yield
         arrive(copies)

time: 115 us -> 113 us (0.983)
  Pallas kernels: 114 us -> 112 us
    pallas_call x1, Pallas kernels: 112 us -> 109 us  [per_device(): pl.pallas_call(kernel, out_shape=shapes, in_specs=[vmem, vmem, anywhere,...]
where the time goes in v4:
time: 113 us
  Pallas kernels  112 us (99%)
    pallas_call x1, Pallas kernels, per_device(): pl.pallas_call(kernel, out_shape=shapes, in_specs=[vmem, vmem, anywhere,...  109 us
    pallas_call x1, Pallas kernels, per_device(): pl.pallas_call(deliver, out_shape=shapes, in_specs=[anywhere] * 3, out_sp...  2.37 us

profile of v4, /device:TPU:1, one launch (start us, length us, event | category | flops | bytes accessed | tf_op | source)
XLA Modules:
  0.0 112.7 jit_solution(15802819273641952801)
XLA Ops:
  0.6 109.5 %shard_map.85 = (bf16[256,384]{1,0:T(8,128)(2,1)}, bf16[128,256]{1,0:T(8,128)(2,1)}, bf16[2048,384]{1,0:T(8,128)(2,1)}) custom-call(s32[2,1,512]{2,1,0:T(1,128)} %bitcast.5, bf16[128,256]{1,0:T(8,128)(2,1)} %slab_ref.1, bf16[256,384]{1,0:T(8,128)(2,1)} %proj_hbm.1, bf16[2048,384]{1,0:T(8,128)(2,1)} %table_ref.1, f32[1188,128]{1,0:T(8,128)} %bitcast.3, ...), custom_call_target="tpu_custom_call" | custom-call | flops 5500000256 | bytes 5000000 | tf_op jit(solution)/shard_map/pallas_call | solution.py:473
  110.1 2.4 %shard_map.86 = (bf16[256,384]{1,0:T(8,128)(2,1)}, bf16[128,256]{1,0:T(8,128)(2,1)}, bf16[2048,384]{1,0:T(8,128)(2,1)}) custom-call(bf16[256,384]{1,0:T(8,128)(2,1)} %get-tuple-element.6.gp_in, bf16[128,256]{1,0:T(8,128)(2,1)} %get-tuple-element.7.gs_in, bf16[2048,384]{1,0:T(8,128)(2,1)} %get-tuple-element.8.gst_in), custom_call_target="tpu_custom_call" | custom-call | tf_op jit(solution)/shard_map/pallas_call | solution.py:522
